TPU v7x, 32 devices: a whole 2x2x4 slice. The times are simulated.
32 devices in a mesh: ctx: 4 (over z), head: 4 (over x, core), row: 2 (over y).
Axes of the slice: x: 2, y: 2, z: 4, core: 2. Of those that a mesh axis runs over, the one named last changes fastest.
Arguments:
- hidden: bfloat16 [384, 8192], P(('ctx', 'row')), may hold values from -6 to 6
- norm_gain: bfloat16 [8192], replicated, may hold values from 0.099609375 to 1.8984375
- q_weight: bfloat16 [8192, 4096], P(None, ('head', 'row')), may hold values from -0.09375 to 0.09375
- q_bias: bfloat16 [4096], P(('head', 'row')), may hold values from -3 to 3
- key_weight: bfloat16 [8192, 512], P(None, 'head'), may hold values from -0.0625 to 0.0625
- key_bias: bfloat16 [512], P('head'), may hold values from -3 to 3
- value_weight: bfloat16 [8192, 512], P(None, 'head'), may hold values from -0.0625 to 0.0625
- value_bias: bfloat16 [512], P('head'), may hold values from -3 to 3
- o_weight: bfloat16 [4096, 8192], P(('head', 'row')), may hold values from -4 to 4
- cached_key_rows: bfloat16 [16384, 512], P('ctx', 'head'), may hold values from -256 to 256
- cached_value_rows: bfloat16 [16384, 512], P('ctx', 'head'), may hold values from -6 to 6
- keep_blocks: int32 [4, 8], P('ctx'), may hold values from 0 to 31, as said below
- kept_counts: int32 [4], replicated, may hold values from 2 to 8, as said below
- span_start: int32 [1], replicated, may hold values from 16384 to 20479
Outputs:
- output: bfloat16 [384, 8192], P('ctx', ('head', 'row'))
Inputs may be any that keep to these rules, and one draw needn't show every extreme that they name: `keep_blocks`: row g lists in increasing order the kept_counts[g] distinct kept blocks among group g's 32 prefix blocks; its remaining entries are 0. `kept_counts`: one group keeps 8 blocks and another keeps 8 // 4.
All inputs are finite; a program needn't handle non-finite values.
Results may differ from a plain program's by a relative error of at most 0.014.
Values may be sent and summed in bfloat16 or wider, within the bound.
No kernel may reach another device: no remote copies, remote signals or barrier semaphores. Data moves between devices by JAX's collectives and lax.ppermute only.
A program may use at most 128 MiB of HBM per device.

v0:
```python
import math

import jax
import jax.numpy as jnp
from jax import lax
from jax.sharding import PartitionSpec as P

BLOCK = 128


def shifted(shard, axis, by):
    peers = lax.axis_size(axis)
    return lax.ppermute(shard, axis, [(i, (i + by) % peers) for i in range(peers)])


def apply_rotary(values, token_positions):
    middle = values.shape[-1] // 2
    steps_range = jnp.arange(middle, dtype=jnp.float32)
    frequency = 1000000.0 ** (-2.0 * steps_range / values.shape[-1])
    angles = token_positions.astype(jnp.float32)[:, None] * frequency[None, :]
    cosine = jnp.cos(angles)[:, None, :]
    sine_part = jnp.sin(angles)[:, None, :]
    first_half = values[..., :middle]
    second_half = values[..., middle:]
    return jnp.concatenate(
        [
            first_half * cosine - second_half * sine_part,
            second_half * cosine + first_half * sine_part,
        ],
        axis=-1,
    )


def local(
    hidden,
    norm_gain,
    q_weight,
    q_bias,
    key_weight,
    key_bias,
    value_weight,
    value_bias,
    o_weight,
    cached_key_rows,
    cached_value_rows,
    keep_blocks,
    kept_counts,
    span_start,
):
    cycle_size = lax.axis_size("ctx")
    group_index = lax.axis_index("ctx")
    row_count = lax.axis_size("row")
    own_rows = hidden.shape[0]
    group_rows = own_rows * row_count
    head_size = key_weight.shape[1]
    query_heads = q_weight.shape[1] // head_size
    query_width = query_heads * head_size
    widened = hidden.astype(jnp.float32)
    rms_factor = lax.rsqrt(jnp.mean(widened * widened, axis=-1, keepdims=True) + 1e-06)
    normed = (widened * rms_factor * norm_gain.astype(jnp.float32)).astype(jnp.bfloat16)
    first_token = span_start[0] + group_index * group_rows
    query_shift = q_bias.astype(jnp.float32)
    key_shift = key_bias.astype(jnp.float32)
    value_shift = value_bias.astype(jnp.float32)
    piece = lax.all_gather(normed, "row", axis=0, tiled=True)
    projected = jnp.dot(piece, q_weight, preferred_element_type=jnp.float32) + query_shift
    key_part = jnp.dot(piece, key_weight, preferred_element_type=jnp.float32) + key_shift
    value_part = jnp.dot(piece, value_weight, preferred_element_type=jnp.float32) + value_shift
    projected = jnp.concatenate([projected, key_part, value_part], axis=1)
    token_positions = first_token + jnp.arange(group_rows, dtype=jnp.int32)
    queries = apply_rotary(
        projected[:, :query_width].reshape(group_rows, query_heads, head_size), token_positions
    ).astype(jnp.bfloat16)
    key_rows = projected[:, query_width : query_width + head_size].reshape(group_rows, 1, head_size)
    span_keys = (
        apply_rotary(key_rows, token_positions).reshape(group_rows, head_size).astype(jnp.bfloat16)
    )
    span_values = projected[:, query_width + head_size :].astype(jnp.bfloat16)
    span_pair = jnp.stack([span_keys, span_values])
    kept_here = keep_blocks[0]
    row_numbers = (
        kept_here[:, None] * BLOCK + jnp.arange(BLOCK, dtype=jnp.int32)[None, :]
    ).reshape(-1)
    prefix_pair = jnp.stack(
        [
            jnp.take(cached_key_rows, row_numbers, axis=0),
            jnp.take(cached_value_rows, row_numbers, axis=0),
        ]
    )
    buffer = jnp.concatenate([prefix_pair, span_pair], axis=1)
    prefix_slots = prefix_pair.shape[1]
    score_scale = 1.0 / math.sqrt(head_size)
    key_position = jnp.arange(buffer.shape[1], dtype=jnp.int32)
    query_token = group_index * group_rows + jnp.arange(group_rows, dtype=jnp.int32)

    def attend_block(carried, travelling, source):
        row_max, denominator, blended = carried
        scores = (
            jnp.einsum("tqd,sd->tqs", queries, travelling[0], preferred_element_type=jnp.float32)
            * score_scale
        )
        live_prefix = key_position // BLOCK < kept_counts[source]
        span_token = source * group_rows + key_position - prefix_slots
        visible = jnp.where(
            key_position[None, :] < prefix_slots,
            live_prefix[None, :],
            span_token[None, :] <= query_token[:, None],
        )
        scores = jnp.where(visible[:, None, :], scores, -jnp.inf)
        new_max = jnp.maximum(row_max, scores.max(axis=-1))
        shrink = jnp.exp(row_max - new_max)
        weights = jnp.exp(scores - new_max[..., None])
        denominator = denominator * shrink + weights.sum(axis=-1)
        blended = blended * shrink[..., None] + jnp.einsum(
            "tqs,sd->tqd",
            weights.astype(jnp.bfloat16),
            travelling[1],
            preferred_element_type=jnp.float32,
        )
        return (new_max, denominator, blended)

    carried = (
        jnp.full((group_rows, query_heads), -jnp.inf, jnp.float32),
        jnp.zeros((group_rows, query_heads), jnp.float32),
        jnp.zeros((group_rows, query_heads, head_size), jnp.float32),
    )
    carried = attend_block(carried, buffer, group_index)

    def forward_step(step_number, loop_state):
        state_now, travelling = loop_state
        travelling = shifted(travelling, "ctx", 1)
        source = (group_index - step_number - 1) % cycle_size
        return (attend_block(state_now, travelling, source), travelling)

    carried, buffer = lax.fori_loop(0, cycle_size - 1, forward_step, (carried, buffer))
    row_max, denominator, blended = carried
    attended = (
        (blended / denominator[..., None]).astype(jnp.bfloat16).reshape(group_rows, query_width)
    )
    summed = lax.psum_scatter(
        lax.dot_general(
            o_weight, attended, (((0,), (1,)), ((), ())), preferred_element_type=jnp.float32
        ),
        ("head", "row"),
        scatter_dimension=0,
        tiled=True,
    )
    result = summed.T.astype(jnp.bfloat16)
    return result


def solution(mesh):
    in_specs = (
        P(("ctx", "row"), None),
        P(),
        P(None, ("head", "row")),
        P(("head", "row")),
        P(None, "head"),
        P("head"),
        P(None, "head"),
        P("head"),
        P(("head", "row"), None),
        P("ctx", "head"),
        P("ctx", "head"),
        P("ctx", None),
        P(),
        P(),
    )
    out_specs = P("ctx", ("head", "row"))
    return jax.shard_map(local, mesh=mesh, in_specs=in_specs, out_specs=out_specs, check_vma=False)
```

profile of v0, /device:TPU:0, one launch (start us, length us, event | category | flops | bytes accessed | tf_op | source)
XLA Modules:
  0.0 164.1 jit_solution(13653517693707899894)
XLA Ops:
  6.6 0.0 all-gather.2.cloned.1.call-start
  6.6 1.5 fusion.18
  8.2 0.7 convert_element_type.65
  8.9 2.3 %fusion.20 = bf16[48,8192]{1,0:T(8,128)(2,1)} fusion(bf16[48,8192]{1,0:T(8,128)(2,1)} %param.18, f32[8192]{0:T(1024)S(1)} %convert_element_type.65, f32[48]{0:T(128)S(1)} %add_rsqrt_fusion), kind=kLoop, calls=%fused_computation.37 | loop fusion | flops 1572864 | bytes 1605824 | tf_op jit(solution)/shard_map/convert_element_type | solution.py:60
  11.2 0.0 all-gather.2.cloned.1.call-update
  11.2 0.0 reduce-scatter.2.cloned.1.call-start
  12.0 0.1 fusion.43
  12.1 3.2 %gather_fusion.1 = bf16[1024,128]{1,0:T(8,128)(2,1)S(1)} fusion(bf16[4096,128]{1,0:T(8,128)(2,1)S(1)} %copy-done.3, s32[1024]{0:T(1024)S(1)} %fusion.43), kind=kCustom, calls=%fused_computation.1.clone | custom fusion | bytes 528384 | tf_op jit(solution)/shard_map/jit(_take)/gather | solution.py:87
  15.3 4.2 %gather_fusion = bf16[1024,128]{1,0:T(8,128)(2,1)S(1)} fusion(bf16[4096,128]{1,0:T(8,128)(2,1)} %param.27, s32[1024]{0:T(1024)S(1)} %fusion.43), kind=kCustom, calls=%fused_computation.clone | custom fusion | bytes 528384 | tf_op jit(solution)/shard_map/jit(_take)/gather | solution.py:86
  19.5 0.6 dynamic_slice.14
  20.1 0.7 fusion.39
  20.8 0.1 fusion.46
  20.9 0.2 multiply_cosine_fusion.1
  21.1 0.2 select_bitcast_fusion.1
  21.3 0.8 compare_select_fusion.1
  22.1 19.1 %all-gather.2.cloned.1.call-done = bf16[96,8192]{1,0:T(8,128)(2,1)} async-done(((bf16[48,8192]{1,0:T(8,128)(2,1)}), bf16[96,8192]{1,0:T(8,128)(2,1)}) %all-gather.2.cloned.1.call-update) | async-done | bytes 1572880 | tf_op jit(solution)/shard_map/all_gather | solution.py:65
  41.3 2.1 %fusion.23 = f32[96,1,128]{2,0,1:T(8,128)S(1)} fusion(bf16[96,8192]{1,0:T(8,128)(2,1)} %all-gather.2.cloned.1.call-done, bf16[8192,128]{1,0:T(8,128)(2,1)S(1)} %copy-done, f32[128]{0:T(128)S(1)} %convert_element_type.69), kind=kOutput, calls=%fused_computation.44 | convolution fusion | flops 201338880 | bytes 3719680 | tf_op jit(solution)/shard_map/dot_general | solution.py:67
  43.4 0.3 fusion.36
  43.7 4.8 %convolution_add_fusion.2 = f32[96,512]{1,0:T(8,128)S(1)} fusion(bf16[96,8192]{1,0:T(8,128)(2,1)S(1)} %copy-done.1, bf16[8192,512]{1,0:T(8,128)(2,1)} %param.20, f32[512]{0:T(512)S(1)} %convert_element_type.67), kind=kOutput, calls=%fused_computation.41 | convolution fusion | flops 805355520 | bytes 10160128 | tf_op jit(solution)/shard_map/dot_general | solution.py:66
  48.5 0.1 reshape.354
  48.6 0.2 fusion.49
  48.8 0.1 maximum_bitcast_fusion
  48.8 0.1 subtract_convert_fusion
  48.9 0.1 pad_maximum_fusion
  49.0 1.0 copy-done.2
  50.0 2.2 %fusion.25 = bf16[1,96,128]{2,1,0:T(8,128)(2,1)S(1)} fusion(bf16[96,8192]{1,0:T(8,128)(2,1)S(1)} %copy-done.2, bf16[8192,128]{1,0:T(8,128)(2,1)} %param.24, f32[128]{0:T(128)S(1)} %convert_element_type.71), kind=kOutput, calls=%fused_computation.46 | convolution fusion | flops 201351168 | bytes 3695104 | tf_op jit(solution)/shard_map/dot_general | solution.py:68
  52.2 0.6 fusion.50
  52.8 0.4 fusion.22
  53.2 0.5 convolution_add_fusion.1
  53.7 51.7 %while.24 = (s32[]{:T(128)}, f32[96,4]{0,1:T(4,128)S(1)}, f32[96,4]{0,1:T(4,128)S(1)}, f32[96,4,128]{2,0,1:T(8,128)S(1)}, bf16[2,1120,128]{2,1,0:T(8,128)(2,1)S(...) while((s32[]{:T(128)}, f32[96,4]{0,1:T(4,128)S(1)}, ...), condition=%wide.region_6.8_spmd.clone.clone, body=%wide.region_3.7_spmd.clone.clone.sunk | while | flops 223539184 | bytes 9976256 | solution.py:135
  53.7 1.5 collective-permute-start
  55.2 0.6 compare_reduce_fusion.2
  55.8 1.3 dynamic_slice.18
  57.2 1.4 iota_compare_fusion.3
  58.5 0.5 iota_add_fusion.4
  59.0 0.8 compare_select_fusion.4
  59.9 10.4 %collective-permute-done = bf16[2,1120,128]{2,1,0:T(8,128)(2,1)S(1)} collective-permute-done((bf16[2,1120,128]{2,1,0:T(8,128)(2,1)S(1)}, bf16[2,1120,128]{2,1,0:T(8,128)(2,1)S(1)}, u32[]{:S(2)}, u32[]{:S(2)}) %collective-permute-start) | collective-permute-done | bytes 573472 | tf_op jit(solution)/shard_map/while/body/eval_jaxpr/ppermute | solution.py:13
  70.3 0.6 fusion.70
  70.8 0.4 fusion.71
  71.3 0.5 convolution_add_fusion.6
  71.8 0.1 collective-permute-start
  71.9 0.6 compare_reduce_fusion.2
  72.5 1.3 dynamic_slice.18
  73.8 1.4 iota_compare_fusion.3
  75.2 0.5 iota_add_fusion.4
  75.7 0.8 compare_select_fusion.4
  76.5 11.0 %collective-permute-done = bf16[2,1120,128]{2,1,0:T(8,128)(2,1)S(1)} collective-permute-done((bf16[2,1120,128]{2,1,0:T(8,128)(2,1)S(1)}, bf16[2,1120,128]{2,1,0:T(8,128)(2,1)S(1)}, u32[]{:S(2)}, u32[]{:S(2)}) %collective-permute-start) | collective-permute-done | bytes 573472 | tf_op jit(solution)/shard_map/while/body/eval_jaxpr/ppermute | solution.py:13
  87.5 0.6 fusion.70
  88.1 0.4 fusion.71
  88.6 0.5 convolution_add_fusion.6
  89.1 0.1 collective-permute-start
  89.1 0.6 compare_reduce_fusion.2
  89.8 1.3 dynamic_slice.18
  91.1 1.4 iota_compare_fusion.3
  92.4 0.5 iota_add_fusion.4
  93.0 0.8 compare_select_fusion.4
  93.8 10.1 %collective-permute-done = bf16[2,1120,128]{2,1,0:T(8,128)(2,1)S(1)} collective-permute-done((bf16[2,1120,128]{2,1,0:T(8,128)(2,1)S(1)}, bf16[2,1120,128]{2,1,0:T(8,128)(2,1)S(1)}, u32[]{:S(2)}, u32[]{:S(2)}) %collective-permute-start) | collective-permute-done | bytes 573472 | tf_op jit(solution)/shard_map/while/body/eval_jaxpr/ppermute | solution.py:13
  103.8 0.6 fusion.70
  104.4 0.4 fusion.71
  104.9 0.5 convolution_add_fusion.6
  105.4 6.6 %convolution_bitcast_fusion = f32[8192,96]{0,1:T(8,128)} fusion(bf16[512,8192]{1,0:T(8,128)(2,1)} %param.26, f32[96,4,128]{2,0,1:T(8,128)S(1)} %get-tuple-element.311, f32[96,4]{0,1:T(4,128)S(1)} %get-tuple-element.312), kind=kOutput, calls=%fused_computation.29 | convolution fusion | flops 805404672 | bytes 11732480 | tf_op jit(solution)/shard_map/dot_general | solution.py:141
  111.9 0.0 reduce-scatter.2.cloned.1.call-update
  112.0 43.6 %reduce-scatter.2.cloned.1.call-done = f32[1024,96]{0,1:T(8,128)} async-done(((f32[8192,96]{0,1:T(8,128)}), f32[1024,96]{0,1:T(8,128)}) %reduce-scatter.2.cloned.1.call-update) | async-done | bytes 393232 | tf_op jit(solution)/shard_map/reduce_scatter | solution.py:140
  155.6 1.7 %convert_bitcast_fusion = bf16[96,1024]{1,0:T(8,128)(2,1)} fusion(f32[1024,96]{0,1:T(8,128)} %reduce-scatter.2.cloned.1.call-done), kind=kLoop, calls=%fused_computation.54 | loop fusion | flops 98304 | bytes 589824 | tf_op jit(solution)/shard_map/convert_element_type | solution.py:148
  (45 shorter events, 0.3 us)
Async XLA Ops:
  6.5 34.7 %copy-start = (bf16[8192,128]{1,0:T(8,128)(2,1)S(1)}, bf16[8192,128]{1,0:T(8,128)(2,1)}, u32[]{:S(2)}) copy-start(bf16[8192,128]{1,0:T(8,128)(2,1)} %param.22) | copy-start | bytes 6291460
  6.5 5.4 %copy-start.6 = (s32[1,8]{1,0:T(1,128)S(1)}, s32[1,8]{1,0:T(1,128)}, u32[]{:S(2)}) copy-start(s32[1,8]{1,0:T(1,128)} %param.29) | copy-start | bytes 100
  6.5 5.4 %copy-start.7 = (bf16[128]{0:T(256)(128)(2,1)S(1)}, bf16[128]{0:T(256)(128)(2,1)}, u32[]{:S(2)}) copy-start(bf16[128]{0:T(256)(128)(2,1)} %param.23) | copy-start | bytes 772
  6.5 5.4 %copy-start.8 = (bf16[128]{0:T(256)(128)(2,1)S(1)}, bf16[128]{0:T(256)(128)(2,1)}, u32[]{:S(2)}) copy-start(bf16[128]{0:T(256)(128)(2,1)} %param.25) | copy-start | bytes 772
  6.5 5.4 %copy-start.5 = (bf16[512]{0:T(512)(128)(2,1)S(1)}, bf16[512]{0:T(512)(128)(2,1)}, u32[]{:S(2)}) copy-start(bf16[512]{0:T(512)(128)(2,1)} %param.21) | copy-start | bytes 3076
  6.5 5.5 %copy-start.3 = (bf16[4096,128]{1,0:T(8,128)(2,1)S(1)}, bf16[4096,128]{1,0:T(8,128)(2,1)}, u32[]{:S(2)}) copy-start(bf16[4096,128]{1,0:T(8,128)(2,1)} %param.28) | copy-start | bytes 3145732
  6.6 34.7 %all-gather.2.cloned.1.call-start = ((), (), s32[]{:S(2)}) async-start(), calls=%async_computation.1 | async-start | bytes 2359296 | tf_op jit(solution)/shard_map/all_gather | solution.py:65
  11.2 144.4 %reduce-scatter.2.cloned.1.call-start = ((), (), s32[]{:S(2)}) async-start(), calls=%async_computation.2 | async-start | bytes 3538944 | tf_op jit(solution)/shard_map/reduce_scatter | solution.py:140
  15.3 4.3 %copy-start.9 = (s32[4]{0:T(128)S(1)}, s32[4]{0:T(128)}, u32[]{:S(2)}) copy-start(s32[4]{0:T(128)} %param.30) | copy-start | bytes 52
  41.3 2.4 %copy-start.1 = (bf16[96,8192]{1,0:T(8,128)(2,1)S(1)}, bf16[96,8192]{1,0:T(8,128)(2,1)}, u32[]{:S(2)}) copy-start(bf16[96,8192]{1,0:T(8,128)(2,1)} %all-gather.2.cloned.1.call-done) | copy-start | bytes 4718596
  48.6 1.4 copy-start.2
  50.0 2.2 %copy-start.4 = (pred[96,1120]{1,0:T(8,128)(4,1)S(1)}, pred[96,1120]{1,0:T(8,128)(4,1)}, u32[]{:S(2)}) copy-start(pred[96,1120]{1,0:T(8,128)(4,1)} %compare_select_fusion.1) | copy-start | bytes 322564
  53.7 16.6 %collective-permute-start = (bf16[2,1120,128]{2,1,0:T(8,128)(2,1)S(1)}, bf16[2,1120,128]{2,1,0:T(8,128)(2,1)S(1)}, u32[]{:S(2)}, u32[]{:S(2)}) collective-permute-start(bf16[2,1120,128]{2,1,0:T(8,128)(2,1)S(1)} %get-tuple-element.492), channel_id=1, source_target_pairs={{0,8},{8,16},{16,24},{24,0},{1,9},{9,17},{17,25},{25,1},{2,10},{10... | collective-permute-start | bytes 1720328 | tf_op jit(solution)/shard_map/while/body/eval_jaxpr/ppermute | solution.py:13
  71.8 15.7 %collective-permute-start = (bf16[2,1120,128]{2,1,0:T(8,128)(2,1)S(1)}, bf16[2,1120,128]{2,1,0:T(8,128)(2,1)S(1)}, u32[]{:S(2)}, u32[]{:S(2)}) collective-permute-start(bf16[2,1120,128]{2,1,0:T(8,128)(2,1)S(1)} %get-tuple-element.492), channel_id=1, source_target_pairs={{0,8},{8,16},{16,24},{24,0},{1,9},{9,17},{17,25},{25,1},{2,10},{10... | collective-permute-start | bytes 1720328 | tf_op jit(solution)/shard_map/while/body/eval_jaxpr/ppermute | solution.py:13
  89.1 14.8 %collective-permute-start = (bf16[2,1120,128]{2,1,0:T(8,128)(2,1)S(1)}, bf16[2,1120,128]{2,1,0:T(8,128)(2,1)S(1)}, u32[]{:S(2)}, u32[]{:S(2)}) collective-permute-start(bf16[2,1120,128]{2,1,0:T(8,128)(2,1)S(1)} %get-tuple-element.492), channel_id=1, source_target_pairs={{0,8},{8,16},{16,24},{24,0},{1,9},{9,17},{17,25},{25,1},{2,10},{10... | collective-permute-start | bytes 1720328 | tf_op jit(solution)/shard_map/while/body/eval_jaxpr/ppermute | solution.py:13
Sparse Core Ops, SparseCore 0:
  11.3 29.9 all-gather.1
  112.1 43.4 reduce-scatter.1
where the time goes:
time: 165 us; the launch traced here: 164 us
  waiting for transfers between devices  94.3 us (57%)
  other arithmetic  20.5 us (12%)
  matrix products  19.8 us (12%)
  between operations  14.3 us (9%)
  local copies, waits for them, and re-layouts  13.3 us (8%)
  starting transfers between devices  1.73 us (1%)
    reduce_scatter x1, waiting for transfers between devices, local(): lax.psum_scatter(lax.dot_general(o_weight, attended, (((0,), (1,)), ((),...  43.6 us
    ppermute x3, waiting for transfers between devices, shifted(): lax.ppermute(shard, axis, [(i, (i + by) % peers) for i in range(peers)])  31.5 us
    all_gather x1, waiting for transfers between devices, local(): piece = lax.all_gather(normed, 'row', axis=0, tiled=True)  19.1 us
    dot_general x1, matrix products, local(): lax.dot_general(o_weight, attended, (((0,), (1,)), ((), ())), preferred_e...  6.56 us
    dot_general x1, matrix products, local(): jnp.dot(piece, q_weight, preferred_element_type=jnp.float32) + query_shift  4.83 us
    dynamic_slice x4, local copies, waits for them, and re-layouts, attend_block(): live_prefix = key_position // BLOCK < kept_counts[source]  4.5 us
    gather x1, local copies, waits for them, and re-layouts, local(): jnp.take(cached_key_rows, row_numbers, axis=0)  4.24 us
    lt x3, other arithmetic, attend_block(): key_position[None, :] < prefix_slots  4.12 us
  transfers between devices with their start and end apart: 5, of which 5 were waited for; matrix products, arithmetic and copies ran while one was open for 15% of the time, Pallas kernels for 0%

commit v1 on v0

v1 whole, which is shorter than its diff:
```python
import functools
import math

import jax
import jax.numpy as jnp
from jax import lax
from jax.experimental import pallas as pl
from jax.experimental.pallas import tpu as pltpu
from jax.sharding import PartitionSpec as P

BLOCK = 128
CORES = 2
COLUMN_PIECES = 8
NORM_ROWS = 16
F32 = jnp.float32
BF16 = jnp.bfloat16
ANYWHERE = pl.BlockSpec(memory_space=pl.ANY)
IN_VMEM = pl.BlockSpec(memory_space=pltpu.VMEM)
IN_SMEM = pl.BlockSpec(memory_space=pltpu.SMEM)
IN_HBM = pl.BlockSpec(memory_space=pltpu.HBM)
VMEM_BYTES = 6 * 1024 * 1024


def params(needed=0):
    return pltpu.CompilerParams(vmem_limit_bytes=VMEM_BYTES + int(needed))


def in_hbm(value):
    return pltpu.with_memory_space_constraint(value, pltpu.HBM)


def in_vmem(value):
    return pltpu.with_memory_space_constraint(value, pltpu.VMEM)


def cost(weight):
    return pl.CostEstimate(flops=weight * 10**8, bytes_accessed=10**4, transcendentals=0)


def run_copies(pairs, sems):
    copies = [
        pltpu.make_async_copy(source, target, sems.at[index])
        for index, (source, target) in enumerate(pairs)
    ]
    for copy in copies:
        copy.start()
    return copies


def column_copies(width, which, weight_ref, out_ref, sems):
    pieces, parts = sems.shape
    depth = out_ref.shape[0] // pieces
    copies = []
    for piece in range(pieces):
        rows = pl.ds(piece * depth, depth)
        pairs = []
        for part in range(parts):
            start = pl.multiple_of((part * CORES + which) * width, width)
            target = out_ref.at[rows, pl.ds(part * width, width)]
            pairs.append((weight_ref.at[rows, pl.ds(start, width)], target))
        copies += run_copies(pairs, sems.at[piece])
    return copies


def piece_row(piece):
    rows = lax.axis_size("row")
    return lax.rem(lax.axis_index("row") + rows - piece, rows)


def first_kernel(
    keep_ref,
    hidden_ref,
    gain_ref,
    keys_ref,
    values_ref,
    normed_ref,
    half_ref,
    prefix_ref,
    raw,
    kept,
    gains,
    row_sems,
    block_sems,
    small_sems,
):
    rows, width = raw.shape
    half = width // CORES
    core = lax.rem(lax.axis_index("head"), CORES)
    slots = keep_ref.shape[1]
    list_copy, gain_copy = run_copies([(keep_ref, kept), (gain_ref, gains)], small_sems)
    steps = [pl.ds(first, NORM_ROWS) for first in range(0, rows, NORM_ROWS)]
    arriving = run_copies([(hidden_ref.at[at, :], raw.at[at, :]) for at in steps], row_sems)
    list_copy.wait()
    pairs = []
    for slot in range(slots):
        block = pl.ds(pl.multiple_of(kept[0, slot] * BLOCK, BLOCK), BLOCK)
        for kind, source in enumerate((keys_ref, values_ref)):
            pairs.append((source.at[block, :], prefix_ref.at[kind, pl.ds(slot * BLOCK, BLOCK), :]))
    others = run_copies(pairs, block_sems)
    gain_copy.wait()
    gain = gains[...].astype(F32)
    lanes = gain.shape[1]
    for copy in arriving:
        copy.wait()
    for at in steps:
        wide = raw[at, :].astype(F32)
        squares = jnp.sum(wide * wide, axis=1, keepdims=True)
        factor = lax.rsqrt(squares * (1.0 / width) + 1e-06)
        for place in range(width // lanes):
            columns = slice(place * lanes, (place + 1) * lanes)
            scaled = wide[:, columns] * factor * gain[place : place + 1, :]
            normed_ref[at, columns] = scaled.astype(BF16)
        half_ref[at, :] = normed_ref[at, pl.ds(pl.multiple_of(core * half, half), half)]
    for copy in others:
        copy.wait()


def first(keep_blocks, hidden, gain, keys, values):
    rows, width = hidden.shape
    slots = keep_blocks.shape[1]
    prefix_shape = (2, slots * BLOCK, keys.shape[1])
    return pl.pallas_call(
        first_kernel,
        out_shape=(
            jax.ShapeDtypeStruct((rows, width), BF16),
            jax.ShapeDtypeStruct((rows, width // CORES), BF16),
            pltpu.VMEM(prefix_shape, BF16),
        ),
        in_specs=[IN_HBM] * 5,
        out_specs=(IN_VMEM,) * 3,
        scratch_shapes=[
            pltpu.VMEM((rows, width), BF16),
            pltpu.SMEM((1, slots), jnp.int32),
            pltpu.VMEM(gain.shape, BF16),
            pltpu.SemaphoreType.DMA((rows // NORM_ROWS,)),
            pltpu.SemaphoreType.DMA((2 * slots,)),
            pltpu.SemaphoreType.DMA((2,)),
        ],
        compiler_params=params(8 * rows * width + 2 * math.prod(prefix_shape)),
        cost_estimate=cost(0),
        name="first",
    )(*(in_hbm(value) for value in (keep_blocks, hidden, gain, keys, values)))


def rotated(values, cosine, sine):
    return (values * cosine + pltpu.roll(values, values.shape[1] // 2, 1) * sine).astype(BF16)


def finish(total, pieces, rows, bias_ref, turn_ref, out_ref, span_ref=None):
    heads, size = bias_ref.shape[0] - 2, bias_ref.shape[1]
    for place, piece in enumerate(pieces):
        turns = pl.ds(pl.multiple_of(piece_row(piece) * rows, 16), rows)
        cosine, sine = turn_ref[0, turns, :], turn_ref[1, turns, :]
        part = total[place * rows : (place + 1) * rows]

        def columns(head):
            return part[:, head * size : (head + 1) * size] + bias_ref[head : head + 1, :]

        for head in range(heads):
            at = (place * heads + head) * rows
            out_ref[at : at + rows, :] = rotated(columns(head), cosine, sine)
        if span_ref is not None:
            span_ref[0] = rotated(columns(heads), cosine, sine)
            span_ref[1] = columns(heads + 1).astype(BF16)


def project_own_kernel(
    chunks,
    normed,
    q_weight,
    key_weight,
    value_weight,
    q_bias,
    key_bias,
    value_bias,
    turn_ref,
    out_ref,
    span_ref,
    weights,
    bias_ref,
    q_raw,
    key_raw,
    value_raw,
    bias_sems,
    sems,
):
    own_rows, width = normed.shape
    depth = width // chunks
    raw = (q_raw, key_raw, value_raw)
    few = run_copies(list(zip((q_bias, key_bias, value_bias), raw, strict=True)), bias_sems)
    copies = []
    for chunk in range(chunks):
        rows = pl.ds(chunk * depth, depth)
        at = 0
        pairs = []
        for source in (q_weight, key_weight, value_weight):
            size = source.shape[1]
            pairs.append((source.at[rows, :], weights.at[rows, pl.ds(at, size)]))
            at += size
        copies.append(run_copies(pairs, sems.at[chunk]))
    total = jnp.zeros((own_rows, weights.shape[1]), F32)
    for chunk in range(chunks):
        for copy in copies[chunk]:
            copy.wait()
        span = slice(chunk * depth, (chunk + 1) * depth)
        total = total + jnp.dot(normed[:, span], weights[span, :], preferred_element_type=F32)
    at = 0
    for copy, bias in zip(few, raw, strict=True):
        copy.wait()
        bias_ref[at : at + bias.shape[0], :] = bias[...].astype(F32)
        at += bias.shape[0]
    finish(total, [0], own_rows, bias_ref, turn_ref, out_ref, span_ref)


def project_own(normed, weights, biases, turns):
    own_rows, width = normed.shape
    heads, head_size = biases[0].shape
    columns = (heads + 2) * head_size
    chunks = 8
    return pl.pallas_call(
        functools.partial(project_own_kernel, chunks),
        out_shape=(
            jax.ShapeDtypeStruct((heads * own_rows, head_size), BF16),
            jax.ShapeDtypeStruct((2, own_rows, head_size), BF16),
            pltpu.VMEM((width, columns), BF16),
            jax.ShapeDtypeStruct((heads + 2, head_size), F32),
        ),
        in_specs=[IN_VMEM] + [IN_HBM] * 6 + [IN_VMEM],
        out_specs=(IN_VMEM,) * 4,
        scratch_shapes=[
            *(pltpu.VMEM(bias.shape, BF16) for bias in biases),
            pltpu.SemaphoreType.DMA((3,)),
            pltpu.SemaphoreType.DMA((chunks, 3)),
        ],
        compiler_params=params(2 * width * columns),
        cost_estimate=cost(200),
        name="project_own",
    )(normed, *(in_hbm(value) for value in (*weights, *biases)), turns)


def half_rows(weights, mine, columns):
    half = weights.shape[0] // CORES
    core = lax.rem(lax.axis_index("head"), CORES)
    first = pl.multiple_of((core if mine else 1 - core) * half, half)
    return weights[pl.ds(first, half), :columns]


def project_near_kernel(near_ref, weights, out_ref):
    out_ref[...] = jnp.dot(
        near_ref[...], half_rows(weights, True, out_ref.shape[1]), preferred_element_type=F32
    )


def project_near(near, weights, columns):
    rows = near.shape[0]
    return pl.pallas_call(
        project_near_kernel,
        out_shape=jax.ShapeDtypeStruct((rows, columns), F32),
        in_specs=[IN_VMEM] * 2,
        out_specs=IN_VMEM,
        compiler_params=params(12 * rows * columns),
        cost_estimate=cost(50),
        name="project_near",
    )(near, in_vmem(weights))


def project_far_kernel(own_rows, far_ref, weights, part_ref, bias_ref, turn_ref, out_ref):
    total = part_ref[...] + jnp.dot(
        far_ref[...], half_rows(weights, False, part_ref.shape[1]), preferred_element_type=F32
    )
    pieces = range(1, far_ref.shape[0] // own_rows + 1)
    finish(total, pieces, own_rows, bias_ref, turn_ref, out_ref)


def project_far(own_rows, far, weights, part, biases, turns):
    rows, columns = part.shape
    head_size = biases.shape[1]
    return pl.pallas_call(
        functools.partial(project_far_kernel, own_rows),
        out_shape=jax.ShapeDtypeStruct((columns // head_size * rows, head_size), BF16),
        in_specs=[IN_VMEM] * 5,
        out_specs=IN_VMEM,
        compiler_params=params(12 * rows * columns),
        cost_estimate=cost(0),
        name="project_far",
    )(far, in_vmem(weights), part, biases, turns)


def pack_rows_kernel(own_ref, near_ref, out_ref):
    out_ref[0] = own_ref[...]
    out_ref[1] = near_ref[...]


def pack_rows(own, near):
    return pl.pallas_call(
        pack_rows_kernel,
        out_shape=jax.ShapeDtypeStruct((2, *own.shape), BF16),
        in_specs=[IN_VMEM] * 2,
        out_specs=IN_VMEM,
        compiler_params=params(),
        cost_estimate=cost(0),
        name="pack_rows",
    )(own, near)


def quotient(values, divisor, most):
    shift = 20
    factor = -(-(1 << shift) // divisor)
    assert all((i * factor) >> shift == i // divisor for i in range(most))
    assert most * factor < 1 << 31
    return lax.shift_right_logical(values * factor, shift)


def token_ids(shape, axis, own_rows, repeats):
    count = shape[axis]
    place = lax.broadcasted_iota(jnp.int32, shape, axis)
    length = own_rows * repeats
    start = jnp.full(shape, piece_row(0) * own_rows, jnp.int32)
    for piece in range(1, count // length):
        start = jnp.where(place >= piece * length, piece_row(piece) * own_rows, start)
    return place - own_rows * quotient(place, own_rows, count) + start


def products(queries, keys):
    return lax.dot_general(queries, keys, (((1,), (1,)), ((), ())), preferred_element_type=F32)


def settle(base, scores, values, top, state=None):
    total = jnp.zeros(top.shape, F32)
    blend = jnp.zeros((top.shape[0], values[0].shape[1]), F32)
    if state is not None:
        shrink = jnp.exp2((state[0] - top) * base)
        total = state[1] * shrink
        blend = state[2] * shrink
    for part, value in zip(scores, values, strict=True):
        weights = jnp.exp2((part - top) * base)
        total = total + jnp.sum(weights, axis=1, keepdims=True)
        blend = blend + jnp.dot(weights.astype(BF16), value, preferred_element_type=F32)
    return top, total, blend


def largest(scores):
    top = None
    for part in scores:
        peak = jnp.max(part, axis=1, keepdims=True)
        top = peak if top is None else jnp.maximum(top, peak)
    return top


def neighbour_group():
    group = lax.axis_index("ctx")
    return group + 1 - 2 * lax.rem(group, 2)


def by_counts(counts_ref, slots, body):
    group, near = lax.axis_index("ctx"), neighbour_group()
    few = slots // 2
    for own_slots in (few, slots):
        for near_slots in (few, slots):
            own_fits = (counts_ref[group] <= few) == (own_slots == few)
            near_fits = (counts_ref[near] <= few) == (near_slots == few)
            pl.when(jnp.logical_and(own_fits, near_fits))(
                functools.partial(body, (own_slots, near_slots))
            )


def prefix_part(queries, counts_ref, prefix_refs, slots):
    scores, values = [], []
    places = (lax.axis_index("ctx"), neighbour_group())
    for group, ref, many in zip(places, prefix_refs, slots, strict=True):
        rows = slice(0, many * BLOCK)
        live = lax.broadcasted_iota(jnp.int32, (1, many * BLOCK), 1) < counts_ref[group] * BLOCK
        scores.append(jnp.where(live, products(queries, ref[0, rows, :]), -jnp.inf))
        values.append(ref[1, rows, :])
    return scores, values


def columns_of(values, rows):
    lane = lax.broadcasted_iota(jnp.int32, (rows, BLOCK), 1)
    tile = jnp.zeros((rows, BLOCK), F32)
    for place, value in enumerate(values):
        tile = jnp.where(lane == place, value, tile)
    return tile


def three_parts(values):
    high = values.astype(BF16).astype(F32)
    middle = (values - high).astype(BF16).astype(F32)
    return [high, middle, (values - high - middle).astype(BF16).astype(F32)]


def tail_rows(count):
    tiles = -(-count // BLOCK)
    return tiles, -(-8 * tiles // 16) * 16


def pack_state(out_ref, top, total, blend):
    count = top.shape[0]
    out_ref[:count, :] = blend.astype(BF16)
    tiles, tail = tail_rows(count)
    tile = columns_of(three_parts(top) + three_parts(total), count)
    if tiles * BLOCK > count:
        tile = jnp.concatenate([tile, jnp.zeros((tiles * BLOCK - count, BLOCK), F32)], axis=0)
    lines = jnp.transpose(tile)[:8]
    rows = [lines[:, i * BLOCK : (i + 1) * BLOCK] for i in range(tiles)]
    if tail > 8 * tiles:
        rows.append(jnp.zeros((tail - 8 * tiles, BLOCK), F32))
    out_ref[count:, :] = jnp.concatenate(rows, axis=0).astype(BF16)


def span_part(span_refs, near, which):
    return jnp.concatenate([ref[near, which] for ref in span_refs], axis=0)


def visit_kernel(base, by, counts_ref, batch_ref, own_prefix, near_prefix, *refs):
    span_refs, out_ref = refs[:-1], refs[-1]
    groups = lax.axis_size("ctx")
    group = lax.axis_index("ctx")
    source = lax.rem(group + groups - by, groups)

    def body(slots):
        queries = batch_ref[...]
        scores, values = prefix_part(queries, counts_ref, (own_prefix, near_prefix), slots)
        for near, place in enumerate((group, neighbour_group())):
            span_scores = products(queries, span_part(span_refs, near, 0))
            scores.append(jnp.where(place < source, span_scores, -jnp.inf))
            values.append(span_part(span_refs, near, 1))
        pack_state(out_ref, *settle(base, scores, values, largest(scores)))

    by_counts(counts_ref, own_prefix.shape[1] // BLOCK, body)


def visit(by, counts, batch, prefixes, spans):
    count, size = batch.shape
    keys = prefixes[0].shape[1] + len(spans) * spans[0].shape[2]
    return pl.pallas_call(
        functools.partial(visit_kernel, math.log2(math.e) / math.sqrt(size), by),
        out_shape=jax.ShapeDtypeStruct((count + tail_rows(count)[1], size), BF16),
        in_specs=[IN_SMEM] + [IN_VMEM] * (3 + len(spans)),
        out_specs=IN_VMEM,
        compiler_params=params(16 * count * keys),
        cost_estimate=cost(1000),
        name="visit",
    )(counts, batch, *prefixes, *spans)


def store_state(out_ref, top, total, blend):
    size = blend.shape[1]
    out_ref[:, :size] = blend
    out_ref[:, size:] = columns_of([top, total], blend.shape[0])


def load_state(ref, rows):
    size = ref.shape[1] - BLOCK
    return ref[rows, size : size + 1], ref[rows, size + 1 : size + 2], ref[rows, :size]


def attend_kernel(base, counts_ref, *refs):
    batch_refs, (own_prefix, near_prefix, out_ref) = refs[:-3], refs[-3:]

    def body(slots):
        queries = jnp.concatenate([ref[...] for ref in batch_refs], axis=0)
        scores, values = prefix_part(queries, counts_ref, (own_prefix, near_prefix), slots)
        store_state(out_ref, *settle(base, scores, values, largest(scores)))

    by_counts(counts_ref, own_prefix.shape[1] // BLOCK, body)


def attend(counts, batches, prefixes):
    size = batches[0].shape[1]
    count = sum(batch.shape[0] for batch in batches)
    return pl.pallas_call(
        functools.partial(attend_kernel, math.log2(math.e) / math.sqrt(size)),
        out_shape=jax.ShapeDtypeStruct((count, size + BLOCK), F32),
        in_specs=[IN_SMEM] + [IN_VMEM] * (2 + len(batches)),
        out_specs=IN_VMEM,
        compiler_params=params(16 * count * prefixes[0].shape[1]),
        cost_estimate=cost(5),
        name="attend",
    )(counts, *batches, *prefixes)


def finish_visit_kernel(base, by, batch_ref, state_ref, *refs):
    span_refs, out_ref = refs[:-1], refs[-1]
    groups = lax.axis_size("ctx")
    group = lax.axis_index("ctx")
    source = lax.rem(group + groups - by, groups)
    queries = batch_ref[...]
    scores, values = [], []
    for near, place in enumerate((group, neighbour_group())):
        span_scores = products(queries, span_part(span_refs, near, 0))
        scores.append(jnp.where(place < source, span_scores, -jnp.inf))
        values.append(span_part(span_refs, near, 1))
    state = load_state(state_ref, slice(None))
    top = jnp.maximum(state[0], largest(scores))
    pack_state(out_ref, *settle(base, scores, values, top, state))


def finish_visit(by, batch, state, spans):
    count, size = batch.shape
    return pl.pallas_call(
        functools.partial(finish_visit_kernel, math.log2(math.e) / math.sqrt(size), by),
        out_shape=jax.ShapeDtypeStruct((count + tail_rows(count)[1], size), BF16),
        in_specs=[IN_VMEM] * (2 + len(spans)),
        out_specs=IN_VMEM,
        compiler_params=params(64 * count * size),
        cost_estimate=cost(1000),
        name="finish_visit",
    )(batch, state, *spans)


def part_state(ref, count):
    tiles, _ = tail_rows(count)
    lines = ref[count:, :].astype(F32)
    lines = jnp.concatenate([lines[8 * i : 8 * i + 8] for i in range(tiles)], axis=1)
    filler = jnp.zeros((BLOCK - 8, tiles * BLOCK), F32)
    tile = jnp.transpose(jnp.concatenate([lines, filler], axis=0))[:count]
    top = tile[:, 0:1] + tile[:, 1:2] + tile[:, 2:3]
    total = tile[:, 3:4] + tile[:, 4:5] + tile[:, 5:6]
    return top, total, ref[:count, :].astype(F32)


def merged(base, parts):
    top = functools.reduce(jnp.maximum, [part[0] for part in parts])
    total, blend = 0.0, 0.0
    for part_top, part_sum, part_blend in parts:
        shrink = jnp.exp2((part_top - top) * base)
        total = total + part_sum * shrink
        blend = blend + part_blend * shrink
    return (blend / total).astype(BF16)


def merge_one_kernel(base, spans, width, one_ref, two_ref, own_ref, own_weight, other_weight, *refs):
    span_refs = refs[:spans]
    state_ref, own_columns, other_columns, sems = refs[spans:]
    core = lax.rem(lax.axis_index("head"), CORES)
    copies = column_copies(width, core, own_weight, own_columns, sems.at[0])
    copies += column_copies(width, core, other_weight, other_columns, sems.at[1])
    total_count = own_ref.shape[0]
    own_rows = span_refs[0].shape[2]
    tokens = spans * own_rows
    group = lax.axis_index("ctx")

    def with_spans(queries, rows):
        query = token_ids((total_count, 1), 0, own_rows, total_count // tokens)
        visible = (token_ids((1, tokens), 1, own_rows, 1) <= query)[rows]
        state = load_state(own_ref, rows)
        scores = [
            jnp.where(visible, products(queries, span_part(span_refs, 0, 0)), -jnp.inf),
            jnp.where(
                neighbour_group() < group, products(queries, span_part(span_refs, 1, 0)), -jnp.inf
            ),
        ]
        values = [span_part(span_refs, near, 1) for near in range(2)]
        top = jnp.maximum(state[0], largest(scores))
        return settle(base, scores, values, top, state)

    @pl.when(group >= 0)
    def _():
        queries = jnp.concatenate([one_ref[...], two_ref[...]], axis=0)
        store_state(state_ref, *with_spans(queries, slice(None)))

    for copy in copies:
        copy.wait()


def merge_one(batches, spans, own, weights, width):
    one, two = batches
    size = one.shape[1]
    shape = (weights[0].shape[0], weights[0].shape[1] // CORES)
    return pl.pallas_call(
        functools.partial(
            merge_one_kernel, math.log2(math.e) / math.sqrt(size), len(spans), width
        ),
        out_shape=(
            jax.ShapeDtypeStruct(own.shape, F32),
            pltpu.VMEM(shape, BF16),
            pltpu.VMEM(shape, BF16),
        ),
        in_specs=[IN_VMEM] * 3 + [IN_HBM, ANYWHERE] + [IN_VMEM] * len(spans),
        out_specs=(IN_VMEM,) * 3,
        scratch_shapes=[pltpu.SemaphoreType.DMA((CORES, COLUMN_PIECES, shape[1] // width))],
        compiler_params=params(64 * own.shape[0] * size + 4 * math.prod(shape)),
        cost_estimate=cost(200),
        name="merge_one",
    )(one, two, own, in_hbm(weights[0]), weights[1], *spans)


def merge_mid_kernel(base, state_ref, *refs):
    part_refs, out_ref = refs[:-1], refs[-1]
    count = out_ref.shape[0]
    parts = [load_state(state_ref, slice(0, count))]
    parts += [part_state(ref, count) for ref in part_refs]
    out_ref[...] = merged(base, parts)


def merge_mid(count, state, parts):
    size = parts[0].shape[1]
    return pl.pallas_call(
        functools.partial(merge_mid_kernel, math.log2(math.e) / math.sqrt(size)),
        out_shape=jax.ShapeDtypeStruct((count, size), BF16),
        in_specs=[IN_VMEM] * (1 + len(parts)),
        out_specs=IN_VMEM,
        compiler_params=params(16 * state.shape[0] * size),
        cost_estimate=cost(100),
        name="merge_mid",
    )(state, *parts)


def merge_two_kernel(base, own_rows, rest_ref, one_ref, *refs):
    part_refs, out_ref = refs[:-1], refs[-1]
    tokens = out_ref.shape[0]
    count, size = one_ref.shape
    heads = count // own_rows
    rest_count = rest_ref.shape[0] - count
    parts = [load_state(rest_ref, slice(count, rest_ref.shape[0]))]
    parts += [part_state(ref, rest_count) for ref in part_refs]
    rest = merged(base, parts)
    for piece in range(tokens // own_rows):
        target = pl.ds(pl.multiple_of(piece_row(piece) * own_rows, 16), own_rows)
        for head in range(heads):
            if piece == 0:
                part = one_ref[head * own_rows : (head + 1) * own_rows, :]
            else:
                at = ((piece - 1) * heads + head) * own_rows
                part = rest[at : at + own_rows]
            out_ref[target, head * size : (head + 1) * size] = part


def merge_two(own_rows, tokens, rest, one, parts):
    count, size = one.shape
    return pl.pallas_call(
        functools.partial(merge_two_kernel, math.log2(math.e) / math.sqrt(size), own_rows),
        out_shape=jax.ShapeDtypeStruct((tokens, count // own_rows * size), BF16),
        in_specs=[IN_VMEM] * (2 + len(parts)),
        out_specs=IN_VMEM,
        compiler_params=params(16 * rest.shape[0] * size),
        cost_estimate=cost(100),
        name="merge_two",
    )(rest, one, *parts)


def block_columns(offsets, width):
    core = lax.rem(lax.axis_index("head"), CORES)
    chip_by, row_by = (
        jnp.where(core == 0, first, second) for first, second in zip(*offsets, strict=True)
    )
    rows = lax.axis_size("row")
    chips = lax.axis_size("head") // CORES
    chip = lax.rem(lax.axis_index("head") // CORES + chip_by, chips)
    row = lax.rem(lax.axis_index("row") + row_by, rows)
    return pl.ds(pl.multiple_of((chip * rows + row) * width, width), width)


def own_share_kernel(offsets, attended_ref, weight, out_ref):
    for place, offset in enumerate(offsets):
        columns = block_columns(offset, out_ref.shape[2])
        out_ref[place] = jnp.dot(
            attended_ref[...], weight[:, columns], preferred_element_type=F32
        )


def own_share(offsets, attended, weight, width):
    shape = (len(offsets), attended.shape[0], width)
    return pl.pallas_call(
        functools.partial(own_share_kernel, offsets),
        out_shape=jax.ShapeDtypeStruct(shape, F32),
        in_specs=[IN_VMEM] * 2,
        out_specs=IN_VMEM,
        compiler_params=params(2 * weight.size + 8 * math.prod(shape)),
        cost_estimate=cost(50),
        name="own_share",
    )(attended, in_vmem(weight))


def out_block_kernel(place, offset, attended_ref, weight, share_ref, out_ref):
    columns = block_columns(offset, out_ref.shape[1])
    block = jnp.dot(attended_ref[...], weight[:, columns], preferred_element_type=F32)
    out_ref[...] = (share_ref[place] + block).astype(out_ref.dtype)


def out_block(place, offset, attended, weight, share, dtype):
    shape = share.shape[1:]
    return pl.pallas_call(
        functools.partial(out_block_kernel, place, offset),
        out_shape=jax.ShapeDtypeStruct(shape, dtype),
        in_specs=[IN_VMEM] * 3,
        out_specs=IN_VMEM,
        compiler_params=params(2 * weight.size + 4 * share.size + 8 * math.prod(shape)),
        cost_estimate=cost(10),
        name="out_block",
    )(attended, in_vmem(weight), share)


def add_block_kernel(total_ref, block_ref, out_ref):
    out_ref[...] = (total_ref[...] + block_ref[...].astype(F32)).astype(out_ref.dtype)


def add_block(total, block, dtype):
    return pl.pallas_call(
        add_block_kernel,
        out_shape=jax.ShapeDtypeStruct(total.shape, dtype),
        in_specs=[IN_VMEM] * 2,
        out_specs=IN_VMEM,
        compiler_params=params(12 * total.size),
        cost_estimate=cost(10),
        name="add_block",
    )(total, block)


def shifted(value, axis, by):
    peers = lax.axis_size(axis)
    return lax.ppermute(value, axis, [(i, (i + by) % peers) for i in range(peers)])


def swapped(value, axis):
    return lax.ppermute(value, axis, [(i, i ^ 1) for i in range(lax.axis_size(axis))])


def local(
    hidden,
    norm_gain,
    q_weight,
    q_bias,
    key_weight,
    key_bias,
    value_weight,
    value_bias,
    o_weight,
    cached_key_rows,
    cached_value_rows,
    keep_blocks,
    kept_counts,
    span_start,
):
    groups = lax.axis_size("ctx")
    rows = lax.axis_size("row")
    chips = lax.axis_size("head") // CORES
    core = lax.axis_index("head") % CORES
    own_rows, width = hidden.shape
    tokens = own_rows * rows
    head_size = key_weight.shape[1]
    block_width = o_weight.shape[1] // (lax.axis_size("head") * rows)
    half = width // CORES

    normed, own_half, own_prefix = first(
        keep_blocks, hidden, norm_gain.reshape(-1, 128), cached_key_rows, cached_value_rows
    )
    near = [shifted(own_half, "row", by) for by in range(1, rows)]
    near = near[0] if rows == 2 else jnp.concatenate(near)
    near_prefix = swapped(own_prefix, "ctx")

    steps = jnp.arange(head_size // 2, dtype=F32)
    frequency = 1000000.0 ** (-2.0 * steps / head_size)
    positions = (
        span_start[0] + lax.axis_index("ctx") * tokens + jnp.arange(tokens, dtype=jnp.int32)
    )
    angles = positions.astype(F32)[:, None] * frequency[None, :]
    cosine, sine = jnp.cos(angles), jnp.sin(angles)
    turns = jnp.stack(
        [jnp.concatenate([cosine, cosine], axis=1), jnp.concatenate([-sine, sine], axis=1)]
    )
    heads = q_weight.shape[1] // head_size
    biases = [bias.reshape(-1, head_size) for bias in (q_bias, key_bias, value_bias)]

    one, span_rows, weights, biases = project_own(
        normed, (q_weight, key_weight, value_weight), biases, turns
    )
    distances = [2 * step for step in range(1, groups // 2)]
    visitors_one = [shifted(one, "ctx", by) for by in distances]
    near_rows = swapped(span_rows, "ctx")
    near, one, span_rows = lax.optimization_barrier((near, one, span_rows))
    far = swapped(near, "head")
    near, o_weight = lax.optimization_barrier((near, o_weight))
    other_weight = swapped(o_weight, "head")
    part = project_near(near, weights, q_weight.shape[1])
    two = project_far(own_rows, far, weights, part, biases, turns)
    visitors_two = [shifted(two, "ctx", by) for by in distances]
    near_rows, two = lax.optimization_barrier((near_rows, two))
    pack = pack_rows(span_rows, near_rows)
    spans = [pack, *(shifted(pack, "row", by) for by in range(1, rows))]

    prefixes = (own_prefix, near_prefix)
    own_state = attend(kept_counts, (one, two), prefixes)
    visitors_one, own_state = lax.optimization_barrier((visitors_one, own_state))
    states = [attend(kept_counts, (visitor,), prefixes) for visitor in visitors_one]
    back_one = [
        finish_visit(by, visitor, state, spans)
        for by, visitor, state in zip(distances, visitors_one, states, strict=True)
    ]
    parts_one = [
        shifted(back, "ctx", -by) for by, back in zip(distances, back_one, strict=True)
    ]
    visitors_two, back_one = lax.optimization_barrier((visitors_two, back_one))
    back_two = [
        visit(by, kept_counts, visitor, prefixes, spans)
        for by, visitor in zip(distances, visitors_two, strict=True)
    ]
    parts_two = [
        shifted(back, "ctx", -by) for by, back in zip(distances, back_two, strict=True)
    ]
    o_weight, other_weight, back_two = lax.optimization_barrier((o_weight, other_weight, back_two))
    state, own_columns, other_columns = merge_one(
        (one, two), spans, own_state, (o_weight, other_weight), rows * block_width
    )
    parts_one, state = lax.optimization_barrier((parts_one, state))
    attended_one = merge_mid(one.shape[0], state, parts_one)
    parts_two, attended_one = lax.optimization_barrier((parts_two, attended_one))
    attended = merge_two(own_rows, tokens, state, attended_one, parts_two)

    other_attended = swapped(attended, "head")
    offsets = [(a, b) for a in range(chips) for b in range(rows)]
    offsets = sorted(offsets[1:], key=lambda offset: (offset[0] != 0) + (offset[1] != 0))
    swapped_offsets = list(offsets)
    for place in range(0, len(offsets) - 1, 2):
        swapped_offsets[place : place + 2] = offsets[place + 1], offsets[place]
    pairs_of_offsets = [*zip(offsets, swapped_offsets, strict=True), ((0, 0), (0, 0))]
    share = own_share(pairs_of_offsets, attended, own_columns, block_width)
    arrived = []
    for place, by_core in enumerate(pairs_of_offsets):
        stays = place == len(offsets)
        block = out_block(
            place, by_core, other_attended, other_columns, share, F32 if stays else BF16
        )
        other_attended, block = lax.optimization_barrier((other_attended, block))
        if stays:
            total = block
            break
        pairs = []
        for c, (chip_by, row_by) in enumerate(by_core):
            for a in range(chips):
                for b in range(rows):
                    target = ((a + chip_by) % chips * CORES + c) * rows + (b + row_by) % rows
                    pairs.append(((a * CORES + c) * rows + b, target))
        arrived.append(lax.ppermute(block, ("head", "row"), pairs))
    for block in arrived[:-1]:
        total = add_block(total, block, F32)
    return add_block(total, arrived[-1], BF16)


def solution(mesh):
    in_specs = (
        P(("ctx", "row"), None),
        P(),
        P(None, ("head", "row")),
        P(("head", "row")),
        P(None, "head"),
        P("head"),
        P(None, "head"),
        P("head"),
        P(("head", "row"), None),
        P("ctx", "head"),
        P("ctx", "head"),
        P("ctx", None),
        P(),
        P(),
    )
    out_specs = P("ctx", ("head", "row"))
    return jax.shard_map(local, mesh=mesh, in_specs=in_specs, out_specs=out_specs, check_vma=False)
```

time: 165 us -> 49.7 us (0.30)
  waiting for transfers between devices: 94.3 us -> 8.52 us
  Pallas kernels: 0 us -> 22.6 us
  other arithmetic: 20.5 us -> 0.37 us
  matrix products: 19.8 us -> 0 us
  starting transfers between devices: 1.73 us -> 17.3 us
  between operations: 14.3 us -> 0.86 us
  local copies, waits for them, and re-layouts: 13.3 us -> 0.01 us
    reduce_scatter x1 -> x0, waiting for transfers between devices: 43.6 us -> none  [local(): lax.psum_scatter(lax.dot_general(o_weight, attended, (((0,), (1,)), ((),...]
    ppermute x3 -> x14, waiting for transfers between devices: 31.5 us -> 8.52 us  [the longest x3 7.14 us: local(): arrived.append(lax.ppermute(block, ('head', 'row'), pairs))]
    pallas_call x0 -> x20, Pallas kernels: none -> 22.6 us  [the longest x1 5.35 us: project_own(): pl.pallas_call(functools.partial(project_own_kernel, chunks), out_shape=(...]
    dot_general x12 -> x0, matrix products: 19.8 us -> none  [the longest x1 6.56 us: local(): lax.dot_general(o_weight, attended, (((0,), (1,)), ((), ())), preferred_e...]
    all_gather x1 -> x0, waiting for transfers between devices: 19.1 us -> none  [local(): piece = lax.all_gather(normed, 'row', axis=0, tiled=True)]
    ppermute x3 -> x14, starting transfers between devices: 1.65 us -> 17.3 us  [the longest x6 11 us: shifted(): lax.ppermute(value, axis, [(i, (i + by) % peers) for i in range(peers)])]
    gather x2 -> x0, local copies, waits for them, and re-layouts: 7.44 us -> none  [the longest x1 4.24 us: local(): jnp.take(cached_key_rows, row_numbers, axis=0)]
    convert_element_type x8 -> x1, other arithmetic: 4.79 us -> 0.01 us  [local(): angles = positions.astype(F32)[:, None] * frequency[None, :]]
  transfers between devices with their start and end apart: 5 -> 14, of which waited for: 5 -> 4; matrix products, arithmetic and copies ran while one was open for 15% -> 1% of each run, Pallas kernels for 0% -> 38%
where the time goes in v1:
time: 49.7 us; the launch traced here: 49.8 us
  Pallas kernels  22.6 us (45%)
  starting transfers between devices  17.3 us (35%)
  waiting for transfers between devices  8.52 us (17%)
  between operations  0.86 us (2%)
    ppermute x6, starting transfers between devices, shifted(): lax.ppermute(value, axis, [(i, (i + by) % peers) for i in range(peers)])  11 us
    ppermute x3, waiting for transfers between devices, local(): arrived.append(lax.ppermute(block, ('head', 'row'), pairs))  7.14 us
    pallas_call x1, Pallas kernels, project_own(): pl.pallas_call(functools.partial(project_own_kernel, chunks), out_shape=(...  5.35 us
    pallas_call x2, Pallas kernels, attend(): pl.pallas_call(functools.partial(attend_kernel, math.log2(math.e) / math....  3.8 us
    ppermute x3, starting transfers between devices, local(): arrived.append(lax.ppermute(block, ('head', 'row'), pairs))  3.68 us
    pallas_call x1, Pallas kernels, merge_one(): pl.pallas_call(functools.partial(merge_one_kernel, math.log2(math.e) / ma...  3.65 us
    ppermute x5, starting transfers between devices, swapped(): lax.ppermute(value, axis, [(i, i ^ 1) for i in range(lax.axis_size(axis))])  2.67 us
    pallas_call x1, Pallas kernels, first(): pl.pallas_call(first_kernel, out_shape=(jax.ShapeDtypeStruct((rows, width...  2.1 us
  transfers between devices with their start and end apart: 14, of which 4 were waited for; matrix products, arithmetic and copies ran while one was open for 1% of the time, Pallas kernels for 38%

profile of v1, /device:TPU:0, one launch (start us, length us, event | category | flops | bytes accessed | tf_op | source)
XLA Modules:
  0.0 49.8 jit_solution(8419987431498556413)
XLA Ops:
  0.0 2.1 %first.1 = (bf16[48,8192]{1,0:T(8,128)(2,1)S(1)}, bf16[48,4096]{1,0:T(8,128)(2,1)S(1)}, bf16[2,1024,128]{2,1,0:T(8,128)(2,1)S(1)}) custom-call(s32[1,8]{1,0:T(1,128)} %keep_ref.1, bf16[48,8192]{1,0:T(8,128)(2,1)} %hidden_ref.1, bf16[64,128]{1,0:T(8,128)(2,1)} %bitcast.10, bf16[4096,128]{1,0:T(8,128)(2,1)} %keys_ref.1, bf16[4096,128]{1,0:T(8,128)(2,1)} %values_ref.1), custom_call_target="tpu_custom_call" | custom-call | bytes 10000 | tf_op jit(solution)/shard_map/first/pallas_call | solution.py:122
  2.1 3.0 %collective-permute-start.1 = (bf16[48,4096]{1,0:T(8,128)(2,1)S(1)}, bf16[48,4096]{1,0:T(8,128)(2,1)S(1)}, u32[]{:S(2)}, u32[]{:S(2)}) collective-permute-start(bf16[48,4096]{1,0:T(8,128)(2,1)S(1)} %get-tuple-element.40), channel_id=1, source_target_pairs={{0,1},{1,0},{2,3},{3,2},{4,5},{5,4},{6,7},{7,6},{8,9},{9,8},{10,11... | collective-permute-start | bytes 1179656 | tf_op jit(solution)/shard_map/ppermute | solution.py:713
  5.1 1.5 %collective-permute-start.4 = (bf16[2,1024,128]{2,1,0:T(8,128)(2,1)S(1)}, bf16[2,1024,128]{2,1,0:T(8,128)(2,1)S(1)}, u32[]{:S(2)}, u32[]{:S(2)}) collective-permute-start(bf16[2,1024,128]{2,1,0:T(8,128)(2,1)S(1)} %get-tuple-element.48.refs_2_.refs_1_.own_prefix), channel_id=1, source_target_pairs={{0,8},{8,0},{16,24},{24,16},{1,9},{9,1},{17,25},{25,17},{2,10},{10... | collective-permute-start | bytes 1572872 | tf_op jit(solution)/shard_map/ppermute | solution.py:717
  7.3 0.3 multiply_cosine_fusion
  7.6 0.1 maximum_bitcast_fusion
  7.7 5.3 %project_own.1 = (bf16[192,128]{1,0:T(8,128)(2,1)S(1)}, bf16[2,48,128]{2,1,0:T(8,128)(2,1)S(1)}, bf16[8192,768]{1,0:T(8,128)(2,1)S(1)}, f32[6,128]{1,0:T(8,128)S(1)}) custom-call(bf16[48,8192]{1,0:T(8,128)(2,1)S(1)} %get-tuple-element.38.normed, bf16[8192,512]{1,0:T(8,128)(2,1)} %q_weight.1, bf16[8192,128]{1,0:T(8,128)(2,1)} %key_weight.1, ...), custom_call_target="tpu_custom_call" | custom-call | flops 20000000000 | bytes 10000 | tf_op jit(solution)/shard_map/project_own/pallas_call | solution.py:220
  13.0 0.0 copy-start
  13.0 0.6 %collective-permute-start.2 = (bf16[2,48,128]{2,1,0:T(8,128)(2,1)S(1)}, bf16[2,48,128]{2,1,0:T(8,128)(2,1)S(1)}, u32[]{:S(2)}, u32[]{:S(2)}) collective-permute-start(bf16[2,48,128]{2,1,0:T(8,128)(2,1)S(1)} %get-tuple-element.50.own_ref), channel_id=1, source_target_pairs={{0,8},{8,0},{16,24},{24,16},{1,9},{9,1},{17,25},{25,17},{2,10},{10... | collective-permute-start | bytes 73736 | tf_op jit(solution)/shard_map/ppermute | solution.py:717
  13.7 2.6 %collective-permute-start = (bf16[192,128]{1,0:T(8,128)(2,1)S(1)}, bf16[192,128]{1,0:T(8,128)(2,1)S(1)}, u32[]{:S(2)}, u32[]{:S(2)}) collective-permute-start(bf16[192,128]{1,0:T(8,128)(2,1)S(1)} %get-tuple-element.42.refs_0_.one_ref), channel_id=1, source_target_pairs={{0,16},{8,24},{16,0},{24,8},{1,17},{9,25},{17,1},{25,9},{2,18},{10... | collective-permute-start | bytes 147464 | tf_op jit(solution)/shard_map/ppermute | solution.py:713
  16.3 0.0 collective-permute-done.1.near_ref
  16.3 0.0 collective-permute-start.3
  16.3 0.5 %collective-permute-start.7 = (bf16[512,8192]{1,0:T(8,128)(2,1)}, bf16[512,8192]{1,0:T(8,128)(2,1)}, u32[]{:S(2)}, u32[]{:S(2)}) collective-permute-start(bf16[512,8192]{1,0:T(8,128)(2,1)} %own_weight), channel_id=1, source_target_pairs={{0,2},{2,0},{4,6},{6,4},{1,3},{3,1},{5,7},{7,5},{8,10},{10,8},{12,... | collective-permute-start | bytes 25165832 | tf_op jit(solution)/shard_map/ppermute | solution.py:717
  16.8 0.8 %project_near.1.part_ref = f32[48,512]{1,0:T(8,128)S(1)} custom-call(bf16[48,4096]{1,0:T(8,128)(2,1)S(1)} %collective-permute-done.1.near_ref, bf16[8192,768]{1,0:T(8,128)(2,1)S(1)} %get-tuple-element.44.weights), custom_call_target="tpu_custom_call" | custom-call | flops 5000000000 | bytes 10000 | tf_op jit(solution)/shard_map/project_near/pallas_call | solution.py:256
  17.6 0.9 %collective-permute-done.3.far_ref = bf16[48,4096]{1,0:T(8,128)(2,1)S(1)} collective-permute-done((bf16[48,4096]{1,0:T(8,128)(2,1)S(1)}, bf16[48,4096]{1,0:T(8,128)(2,1)S(1)}, u32[]{:S(2)}, u32[]{:S(2)}) %collective-permute-start.3) | collective-permute-done | bytes 393248 | tf_op jit(solution)/shard_map/ppermute | solution.py:717
  18.5 0.0 copy-start.2
  18.5 0.9 %project_far.1.refs_1_.two_ref = bf16[192,128]{1,0:T(8,128)(2,1)S(1)} custom-call(bf16[48,4096]{1,0:T(8,128)(2,1)S(1)} %collective-permute-done.3.far_ref, bf16[8192,768]{1,0:T(8,128)(2,1)S(1)} %get-tuple-element.44.weights, f32[48,512]{1,0:T(8,128)S(1)} %project_near.1.part_ref, f32[6,128]{1,0:T(8,128)S(1)} %get-tuple-element.46.bias_ref, ...), custom_call_target="tpu_custom_call" | custom-call | bytes 10000 | tf_op jit(solution)/shard_map/project_far/pallas_call | solution.py:278
  19.5 0.9 %collective-permute-start.8 = (bf16[192,128]{1,0:T(8,128)(2,1)S(1)}, bf16[192,128]{1,0:T(8,128)(2,1)S(1)}, u32[]{:S(2)}, u32[]{:S(2)}) collective-permute-start(bf16[192,128]{1,0:T(8,128)(2,1)S(1)} %project_far.1.refs_1_.two_ref), channel_id=1, source_target_pairs={{0,16},{8,24},{16,0},{24,8},{1,17},{9,25},{17,1},{25,9},{2,18},{10... | collective-permute-start | bytes 147464 | tf_op jit(solution)/shard_map/ppermute | solution.py:713
  20.4 0.0 collective-permute-done.2.near_ref
  20.4 1.6 %collective-permute-start.5 = (bf16[2,2,48,128]{3,2,1,0:T(8,128)(2,1)S(1)}, bf16[2,2,48,128]{3,2,1,0:T(8,128)(2,1)S(1)}, u32[]{:S(2)}, u32[]{:S(2)}) collective-permute-start(bf16[2,2,48,128]{3,2,1,0:T(8,128)(2,1)S(1)} %pack_rows.1.refs_0_), channel_id=1, source_target_pairs={{0,1},{1,0},{2,3},{3,2},{4,5},{5,4},{6,7},{7,6},{8,9},{9,8},{10,11... | collective-permute-start | bytes 147464 | tf_op jit(solution)/shard_map/ppermute | solution.py:713
  21.9 0.0 collective-permute-done.4.refs_3_.refs_2_.near_prefix
  21.9 0.0 copy-done
  22.0 0.0 copy-done.2
  22.0 2.3 %attend.2.own_ref = f32[384,256]{1,0:T(8,128)S(1)} custom-call(s32[4]{0:T(128)S(1)} %copy-done.2, bf16[192,128]{1,0:T(8,128)(2,1)S(1)} %get-tuple-element.42.refs_0_.one_ref, bf16[192,128]{1,0:T(8,128)(2,1)S(1)} %project_far.1.refs_1_.two_ref, bf16[2,1024,128]{2,1,0:T(8,128)(2,1)S(1)} %get-tuple-element.48.refs_2_.refs_1_.own_prefix, ...), custom_call_target="tpu_custom_call" | custom-call | flops 500000000 | bytes 10000 | tf_op jit(solution)/shard_map/attend/pallas_call | solution.py:472
  24.3 0.0 collective-permute-done.refs_0_.batch_ref
  24.3 1.5 %attend.3.state_ref = f32[192,256]{1,0:T(8,128)S(1)} custom-call(s32[4]{0:T(128)S(1)} %copy-done.2, bf16[192,128]{1,0:T(8,128)(2,1)S(1)} %collective-permute-done.refs_0_.batch_ref, bf16[2,1024,128]{2,1,0:T(8,128)(2,1)S(1)} %get-tuple-element.48.refs_2_.refs_1_.own_prefix, bf16[2,1024,128]{2,1,0:T(8,128)(2,1)S(1)} %collective-permute-done.4.refs_3_.refs_2_.near_prefix), custom_call_target="tpu_custom_call" | custom-call | flops 500000000 | bytes 10000 | tf_op jit(solution)/shard_map/attend/pallas_call | solution.py:472
  25.8 0.0 collective-permute-done.5.refs_1_
  25.8 0.7 %finish_visit.1 = bf16[208,128]{1,0:T(8,128)(2,1)S(1)} custom-call(bf16[192,128]{1,0:T(8,128)(2,1)S(1)} %collective-permute-done.refs_0_.batch_ref, f32[192,256]{1,0:T(8,128)S(1)} %attend.3.state_ref, bf16[2,2,48,128]{3,2,1,0:T(8,128)(2,1)S(1)} %pack_rows.1.refs_0_, bf16[2,2,48,128]{3,2,1,0:T(8,128)(2,1)S(1)} %collective-permute-done.5.refs_1_), custom_call_target="tpu_custom_call" | custom-call | flops 99999997952 | bytes 10000 | tf_op jit(solution)/shard_map/finish_visit/pallas_call | solution.py:501
  26.4 0.0 copy-start.1
  26.4 0.9 %collective-permute-start.6 = (bf16[208,128]{1,0:T(8,128)(2,1)S(1)}, bf16[208,128]{1,0:T(8,128)(2,1)S(1)}, u32[]{:S(2)}, u32[]{:S(2)}) collective-permute-start(bf16[208,128]{1,0:T(8,128)(2,1)S(1)} %finish_visit.1), channel_id=1, source_target_pairs={{0,16},{8,24},{16,0},{24,8},{1,17},{9,25},{17,1},{25,9},{2,18},{10... | collective-permute-start | bytes 159752 | tf_op jit(solution)/shard_map/ppermute | solution.py:713
  27.3 0.0 collective-permute-done.8.batch_ref
  27.3 1.5 %visit.1 = bf16[208,128]{1,0:T(8,128)(2,1)S(1)} custom-call(s32[4]{0:T(128)S(1)} %copy-done.2, bf16[192,128]{1,0:T(8,128)(2,1)S(1)} %collective-permute-done.8.batch_ref, bf16[2,1024,128]{2,1,0:T(8,128)(2,1)S(1)} %get-tuple-element.48.refs_2_.refs_1_.own_prefix, bf16[2,1024,128]{2,1,0:T(8,128)(2,1)S(1)} %collective-permute-done.4.refs_3_.refs_2_.near_prefix, ...), custom_call_target="tpu_custom_call" | custom-call | flops 99999997952 | bytes 10000 | tf_op jit(solution)/shard_map/visit/pallas_call | solution.py:436
  28.8 2.0 %collective-permute-start.9 = (bf16[208,128]{1,0:T(8,128)(2,1)S(1)}, bf16[208,128]{1,0:T(8,128)(2,1)S(1)}, u32[]{:S(2)}, u32[]{:S(2)}) collective-permute-start(bf16[208,128]{1,0:T(8,128)(2,1)S(1)} %visit.1), channel_id=1, source_target_pairs={{0,16},{8,24},{16,0},{24,8},{1,17},{9,25},{17,1},{25,9},{2,18},{10... | collective-permute-start | bytes 159752 | tf_op jit(solution)/shard_map/ppermute | solution.py:713
  30.8 0.0 collective-permute-done.7.other_weight
  30.8 0.0 copy-done.1
  30.8 3.7 %merge_one.1 = (f32[384,256]{1,0:T(8,128)S(1)}, bf16[512,4096]{1,0:T(8,128)(2,1)S(1)}, bf16[512,4096]{1,0:T(8,128)(2,1)S(1)}) custom-call(bf16[192,128]{1,0:T(8,128)(2,1)S(1)} %copy-done.1, bf16[192,128]{1,0:T(8,128)(2,1)S(1)} %project_far.1.refs_1_.two_ref, f32[384,256]{1,0:T(8,128)S(1)} %attend.2.own_ref, bf16[512,8192]{1,0:T(8,128)(2,1)} %own_weight, ...), custom_call_target="tpu_custom_call" | custom-call | flops 20000000000 | bytes 10000 | tf_op jit(solution)/shard_map/merge_one/pallas_call | solution.py:571
  34.5 0.0 collective-permute-done.6.refs_0_
  34.5 0.5 %merge_mid.1.one_ref = bf16[192,128]{1,0:T(8,128)(2,1)S(1)} custom-call(f32[384,256]{1,0:T(8,128)S(1)} %get-tuple-element.58.state_ref.rest_ref, bf16[208,128]{1,0:T(8,128)(2,1)S(1)} %collective-permute-done.6.refs_0_), custom_call_target="tpu_custom_call" | custom-call | flops 10000000000 | bytes 10000 | tf_op jit(solution)/shard_map/merge_mid/pallas_call | solution.py:599
  35.0 0.0 collective-permute-done.9.refs_0_
  35.0 0.5 %merge_two.1.attended_ref = bf16[96,512]{1,0:T(8,128)(2,1)S(1)} custom-call(f32[384,256]{1,0:T(8,128)S(1)} %get-tuple-element.58.state_ref.rest_ref, bf16[192,128]{1,0:T(8,128)(2,1)S(1)} %merge_mid.1.one_ref, bf16[208,128]{1,0:T(8,128)(2,1)S(1)} %collective-permute-done.9.refs_0_), custom_call_target="tpu_custom_call" | custom-call | flops 10000000000 | bytes 10000 | tf_op jit(solution)/shard_map/merge_two/pallas_call | solution.py:632
  35.5 0.1 collective-permute-start.10
  35.6 0.8 %own_share.1.share_ref = f32[4,96,1024]{2,1,0:T(8,128)S(1)} custom-call(bf16[96,512]{1,0:T(8,128)(2,1)S(1)} %merge_two.1.attended_ref, bf16[512,4096]{1,0:T(8,128)(2,1)S(1)} %get-tuple-element.63.weight), custom_call_target="tpu_custom_call" | custom-call | flops 5000000000 | bytes 10000 | tf_op jit(solution)/shard_map/own_share/pallas_call | solution.py:665
  36.4 0.5 collective-permute-done.10.attended_ref
  36.9 0.3 out_block.4
  37.2 0.6 %collective-permute-start.11 = (bf16[96,1024]{1,0:T(8,128)(2,1)S(1)}, bf16[96,1024]{1,0:T(8,128)(2,1)S(1)}, u32[]{:S(2)}, u32[]{:S(2)}) collective-permute-start(bf16[96,1024]{1,0:T(8,128)(2,1)S(1)} %out_block.4), channel_id=1, source_target_pairs={{0,1},{1,0},{4,5},{5,4},{2,6},{3,7},{6,2},{7,3},{8,9},{9,8},{12,13... | collective-permute-start | bytes 589832 | tf_op jit(solution)/shard_map/ppermute | solution.py:835
  37.8 0.3 out_block.5
  38.1 1.6 %collective-permute-start.12 = (bf16[96,1024]{1,0:T(8,128)(2,1)S(1)}, bf16[96,1024]{1,0:T(8,128)(2,1)S(1)}, u32[]{:S(2)}, u32[]{:S(2)}) collective-permute-start(bf16[96,1024]{1,0:T(8,128)(2,1)S(1)} %out_block.5), channel_id=1, source_target_pairs={{0,4},{1,5},{4,0},{5,1},{2,3},{3,2},{6,7},{7,6},{8,12},{9,13},{12,... | collective-permute-start | bytes 589832 | tf_op jit(solution)/shard_map/ppermute | solution.py:835
  39.6 0.3 out_block.6
  39.9 1.5 %collective-permute-start.13 = (bf16[96,1024]{1,0:T(8,128)(2,1)S(1)}, bf16[96,1024]{1,0:T(8,128)(2,1)S(1)}, u32[]{:S(2)}, u32[]{:S(2)}) collective-permute-start(bf16[96,1024]{1,0:T(8,128)(2,1)S(1)} %out_block.6), channel_id=1, source_target_pairs={{0,5},{1,4},{4,1},{5,0},{2,7},{3,6},{6,3},{7,2},{8,13},{9,12},{12,... | collective-permute-start | bytes 589832 | tf_op jit(solution)/shard_map/ppermute | solution.py:835
  41.5 0.3 out_block.7.total_ref
  41.8 3.8 %collective-permute-done.11.block_ref = bf16[96,1024]{1,0:T(8,128)(2,1)S(1)} collective-permute-done((bf16[96,1024]{1,0:T(8,128)(2,1)S(1)}, bf16[96,1024]{1,0:T(8,128)(2,1)S(1)}, u32[]{:S(2)}, u32[]{:S(2)}) %collective-permute-start.11) | collective-permute-done | bytes 196640 | tf_op jit(solution)/shard_map/ppermute | solution.py:835
  45.6 0.0 collective-permute-done.12.block_ref
  45.7 3.4 %collective-permute-done.13.block_ref = bf16[96,1024]{1,0:T(8,128)(2,1)S(1)} collective-permute-done((bf16[96,1024]{1,0:T(8,128)(2,1)S(1)}, bf16[96,1024]{1,0:T(8,128)(2,1)S(1)}, u32[]{:S(2)}, u32[]{:S(2)}) %collective-permute-start.13) | collective-permute-done | bytes 196640 | tf_op jit(solution)/shard_map/ppermute | solution.py:835
  49.0 0.7 %add_block.5 = bf16[96,1024]{1,0:T(8,128)(2,1)} custom-call(f32[96,1024]{1,0:T(8,128)S(1)} %add_block.4.total_ref, bf16[96,1024]{1,0:T(8,128)(2,1)S(1)} %collective-permute-done.13.block_ref), custom_call_target="tpu_custom_call" | custom-call | flops 1000000000 | bytes 10000 | tf_op jit(solution)/shard_map/add_block/pallas_call | solution.py:700
  (6 shorter events, 0.1 us)
Async XLA Ops:
  2.1 14.2 %collective-permute-start.1 = (bf16[48,4096]{1,0:T(8,128)(2,1)S(1)}, bf16[48,4096]{1,0:T(8,128)(2,1)S(1)}, u32[]{:S(2)}, u32[]{:S(2)}) collective-permute-start(bf16[48,4096]{1,0:T(8,128)(2,1)S(1)} %get-tuple-element.40), channel_id=1, source_target_pairs={{0,1},{1,0},{2,3},{3,2},{4,5},{5,4},{6,7},{7,6},{8,9},{9,8},{10,11... | collective-permute-start | bytes 1179656 | tf_op jit(solution)/shard_map/ppermute | solution.py:713
  5.1 16.8 %collective-permute-start.4 = (bf16[2,1024,128]{2,1,0:T(8,128)(2,1)S(1)}, bf16[2,1024,128]{2,1,0:T(8,128)(2,1)S(1)}, u32[]{:S(2)}, u32[]{:S(2)}) collective-permute-start(bf16[2,1024,128]{2,1,0:T(8,128)(2,1)S(1)} %get-tuple-element.48.refs_2_.refs_1_.own_prefix), channel_id=1, source_target_pairs={{0,8},{8,0},{16,24},{24,16},{1,9},{9,1},{17,25},{25,17},{2,10},{10... | collective-permute-start | bytes 1572872 | tf_op jit(solution)/shard_map/ppermute | solution.py:717
  13.0 8.9 %copy-start = (bf16[192,128]{1,0:T(8,128)(2,1)}, bf16[192,128]{1,0:T(8,128)(2,1)S(1)}, u32[]{:S(2)}) copy-start(bf16[192,128]{1,0:T(8,128)(2,1)S(1)} %get-tuple-element.42.refs_0_.one_ref) | copy-start | bytes 147460
  13.0 7.3 %collective-permute-start.2 = (bf16[2,48,128]{2,1,0:T(8,128)(2,1)S(1)}, bf16[2,48,128]{2,1,0:T(8,128)(2,1)S(1)}, u32[]{:S(2)}, u32[]{:S(2)}) collective-permute-start(bf16[2,48,128]{2,1,0:T(8,128)(2,1)S(1)} %get-tuple-element.50.own_ref), channel_id=1, source_target_pairs={{0,8},{8,0},{16,24},{24,16},{1,9},{9,1},{17,25},{25,17},{2,10},{10... | collective-permute-start | bytes 73736 | tf_op jit(solution)/shard_map/ppermute | solution.py:717
  13.7 10.6 %collective-permute-start = (bf16[192,128]{1,0:T(8,128)(2,1)S(1)}, bf16[192,128]{1,0:T(8,128)(2,1)S(1)}, u32[]{:S(2)}, u32[]{:S(2)}) collective-permute-start(bf16[192,128]{1,0:T(8,128)(2,1)S(1)} %get-tuple-element.42.refs_0_.one_ref), channel_id=1, source_target_pairs={{0,16},{8,24},{16,0},{24,8},{1,17},{9,25},{17,1},{25,9},{2,18},{10... | collective-permute-start | bytes 147464 | tf_op jit(solution)/shard_map/ppermute | solution.py:713
  16.3 2.2 %collective-permute-start.3 = (bf16[48,4096]{1,0:T(8,128)(2,1)S(1)}, bf16[48,4096]{1,0:T(8,128)(2,1)S(1)}, u32[]{:S(2)}, u32[]{:S(2)}) collective-permute-start(bf16[48,4096]{1,0:T(8,128)(2,1)S(1)} %collective-permute-done.1.near_ref), channel_id=1, source_target_pairs={{0,2},{2,0},{4,6},{6,4},{1,3},{3,1},{5,7},{7,5},{8,10},{10,8},{12,... | collective-permute-start | bytes 1179656 | tf_op jit(solution)/shard_map/ppermute | solution.py:717
  16.3 14.5 %collective-permute-start.7 = (bf16[512,8192]{1,0:T(8,128)(2,1)}, bf16[512,8192]{1,0:T(8,128)(2,1)}, u32[]{:S(2)}, u32[]{:S(2)}) collective-permute-start(bf16[512,8192]{1,0:T(8,128)(2,1)} %own_weight), channel_id=1, source_target_pairs={{0,2},{2,0},{4,6},{6,4},{1,3},{3,1},{5,7},{7,5},{8,10},{10,8},{12,... | collective-permute-start | bytes 25165832 | tf_op jit(solution)/shard_map/ppermute | solution.py:717
  18.5 3.4 %copy-start.2 = (s32[4]{0:T(128)S(1)}, s32[4]{0:T(128)}, u32[]{:S(2)}) copy-start(s32[4]{0:T(128)} %counts_ref.5) | copy-start | bytes 52
  19.5 7.9 %collective-permute-start.8 = (bf16[192,128]{1,0:T(8,128)(2,1)S(1)}, bf16[192,128]{1,0:T(8,128)(2,1)S(1)}, u32[]{:S(2)}, u32[]{:S(2)}) collective-permute-start(bf16[192,128]{1,0:T(8,128)(2,1)S(1)} %project_far.1.refs_1_.two_ref), channel_id=1, source_target_pairs={{0,16},{8,24},{16,0},{24,8},{1,17},{9,25},{17,1},{25,9},{2,18},{10... | collective-permute-start | bytes 147464 | tf_op jit(solution)/shard_map/ppermute | solution.py:713
  20.4 5.4 %collective-permute-start.5 = (bf16[2,2,48,128]{3,2,1,0:T(8,128)(2,1)S(1)}, bf16[2,2,48,128]{3,2,1,0:T(8,128)(2,1)S(1)}, u32[]{:S(2)}, u32[]{:S(2)}) collective-permute-start(bf16[2,2,48,128]{3,2,1,0:T(8,128)(2,1)S(1)} %pack_rows.1.refs_0_), channel_id=1, source_target_pairs={{0,1},{1,0},{2,3},{3,2},{4,5},{5,4},{6,7},{7,6},{8,9},{9,8},{10,11... | collective-permute-start | bytes 147464 | tf_op jit(solution)/shard_map/ppermute | solution.py:713
  26.4 4.4 %copy-start.1 = (bf16[192,128]{1,0:T(8,128)(2,1)S(1)}, bf16[192,128]{1,0:T(8,128)(2,1)}, u32[]{:S(2)}) copy-start(bf16[192,128]{1,0:T(8,128)(2,1)} %copy-done) | copy-start | bytes 147460
  26.4 8.0 %collective-permute-start.6 = (bf16[208,128]{1,0:T(8,128)(2,1)S(1)}, bf16[208,128]{1,0:T(8,128)(2,1)S(1)}, u32[]{:S(2)}, u32[]{:S(2)}) collective-permute-start(bf16[208,128]{1,0:T(8,128)(2,1)S(1)} %finish_visit.1), channel_id=1, source_target_pairs={{0,16},{8,24},{16,0},{24,8},{1,17},{9,25},{17,1},{25,9},{2,18},{10... | collective-permute-start | bytes 159752 | tf_op jit(solution)/shard_map/ppermute | solution.py:713
  28.8 6.2 %collective-permute-start.9 = (bf16[208,128]{1,0:T(8,128)(2,1)S(1)}, bf16[208,128]{1,0:T(8,128)(2,1)S(1)}, u32[]{:S(2)}, u32[]{:S(2)}) collective-permute-start(bf16[208,128]{1,0:T(8,128)(2,1)S(1)} %visit.1), channel_id=1, source_target_pairs={{0,16},{8,24},{16,0},{24,8},{1,17},{9,25},{17,1},{25,9},{2,18},{10... | collective-permute-start | bytes 159752 | tf_op jit(solution)/shard_map/ppermute | solution.py:713
  35.5 1.4 %collective-permute-start.10 = (bf16[96,512]{1,0:T(8,128)(2,1)S(1)}, bf16[96,512]{1,0:T(8,128)(2,1)S(1)}, u32[]{:S(2)}, u32[]{:S(2)}) collective-permute-start(bf16[96,512]{1,0:T(8,128)(2,1)S(1)} %merge_two.1.attended_ref), channel_id=1, source_target_pairs={{0,2},{2,0},{4,6},{6,4},{1,3},{3,1},{5,7},{7,5},{8,10},{10,8},{12,... | collective-permute-start | bytes 294920 | tf_op jit(solution)/shard_map/ppermute | solution.py:717
  37.2 8.4 %collective-permute-start.11 = (bf16[96,1024]{1,0:T(8,128)(2,1)S(1)}, bf16[96,1024]{1,0:T(8,128)(2,1)S(1)}, u32[]{:S(2)}, u32[]{:S(2)}) collective-permute-start(bf16[96,1024]{1,0:T(8,128)(2,1)S(1)} %out_block.4), channel_id=1, source_target_pairs={{0,1},{1,0},{4,5},{5,4},{2,6},{3,7},{6,2},{7,3},{8,9},{9,8},{12,13... | collective-permute-start | bytes 589832 | tf_op jit(solution)/shard_map/ppermute | solution.py:835
  38.1 7.5 %collective-permute-start.12 = (bf16[96,1024]{1,0:T(8,128)(2,1)S(1)}, bf16[96,1024]{1,0:T(8,128)(2,1)S(1)}, u32[]{:S(2)}, u32[]{:S(2)}) collective-permute-start(bf16[96,1024]{1,0:T(8,128)(2,1)S(1)} %out_block.5), channel_id=1, source_target_pairs={{0,4},{1,5},{4,0},{5,1},{2,3},{3,2},{6,7},{7,6},{8,12},{9,13},{12,... | collective-permute-start | bytes 589832 | tf_op jit(solution)/shard_map/ppermute | solution.py:835
  39.9 9.1 %collective-permute-start.13 = (bf16[96,1024]{1,0:T(8,128)(2,1)S(1)}, bf16[96,1024]{1,0:T(8,128)(2,1)S(1)}, u32[]{:S(2)}, u32[]{:S(2)}) collective-permute-start(bf16[96,1024]{1,0:T(8,128)(2,1)S(1)} %out_block.6), channel_id=1, source_target_pairs={{0,5},{1,4},{4,1},{5,0},{2,7},{3,6},{6,3},{7,2},{8,13},{9,12},{12,... | collective-permute-start | bytes 589832 | tf_op jit(solution)/shard_map/ppermute | solution.py:835
